TPU v7x, 512 devices: a whole 4x4x16 slice. The times are simulated.
512 devices in a mesh: section: 32 (over z, core), tensor: 8 (over x, y_lo), replica: 2 (over y_hi).
Axes of the slice: x: 4, y: 4 (y_hi: 2, y_lo: 2; y = y_hi * 2 + y_lo), z: 16, core: 2. Of those that a mesh axis runs over, the one named last changes fastest.
Arguments:
- pool_inputs: bfloat16 [32, 256, 2, 1408], P('section', 'replica', None, 'tensor'), may hold values from -6 to 6
- pool_mixed: bfloat16 [32, 256, 1408], P('section', 'replica'), may hold values from -6 to 6
- crop_ids: int32 [32, 8, 128], P('section', 'replica'), may hold values from 0 to 127
- incoming: bfloat16 [32, 256, 1408], P('section', 'replica', 'tensor'), may hold values from -6 to 6
- loss_grads: bfloat16 [3, 256, 1408], P(None, 'replica', 'tensor'), may hold values from -6 to 6
- w_proj: bfloat16 [32, 2, 1408, 1408], P('section', None, ('tensor', 'replica')), may hold values from -0.109375 to 0.109375
- w_up: bfloat16 [32, 1408, 3072], P('section', None, ('tensor', 'replica')), may hold values from -0.15625 to 0.15625
- w_down: bfloat16 [32, 3072, 1408], P('section', ('tensor', 'replica')), may hold values from -0.109375 to 0.109375
Outputs:
- grad_proj: bfloat16 [32, 2, 1408, 1408], P('section', None, ('tensor', 'replica'))
- grad_up: bfloat16 [32, 1408, 3072], P('section', None, ('tensor', 'replica'))
- grad_down: bfloat16 [32, 3072, 1408], P('section', ('tensor', 'replica'))
- outgoing: bfloat16 [32, 256, 2, 1408], P('section', 'replica', None, 'tensor')
All inputs are finite; a program needn't handle non-finite values.
Results may differ from a plain program's by a relative error of at most 0.02.
Values may be sent and summed in bfloat16 or wider, within the bound.
No kernel may reach another device: no remote copies, remote signals or barrier semaphores. Data moves between devices by JAX's collectives and lax.ppermute only.
A program may use at most 64 MiB of HBM per device.

v0:
```python
import jax
import jax.numpy as jnp
from jax import lax
from jax.sharding import PartitionSpec as P

gelu_scale = 0.7978845608
gelu_cubic = 0.044715


def from_partner(value, axis, bit):
    mask = 2**bit
    pairs = [(source, source ^ mask) for source in range(lax.axis_size(axis))]
    return lax.ppermute(value, axis, pairs)


def shifted(x, axis, by):
    devices = lax.axis_size(axis)
    pairs = [(i, i + by) for i in range(devices) if 0 <= i + by < devices]
    return lax.ppermute(x, axis, pairs)


def gelu_pair(pre_gelu):
    inner = gelu_scale * (pre_gelu + gelu_cubic * pre_gelu * pre_gelu * pre_gelu)
    tanh_part = jnp.tanh(inner)
    gelu_value = 0.5 * pre_gelu * (1.0 + tanh_part)
    gelu_slope = 0.5 * (1.0 + tanh_part) + 0.5 * pre_gelu * (
        1.0 - tanh_part * tanh_part
    ) * gelu_scale * (1.0 + 3.0 * gelu_cubic * pre_gelu * pre_gelu)
    return (gelu_value, gelu_slope)


def reflect(block, section_count):
    for bit_number in range(section_count.bit_length() - 1):
        block = from_partner(block, "section", bit_number)
    return block


def body(pool_inputs, pool_mixed, crop_ids, incoming, loss_grads, w_proj, w_up, w_down):
    section_index = lax.axis_index("section")
    section_count = lax.axis_size("section")
    proj_full, up_full, down_full = (
        lax.all_gather(w_proj, "replica", axis=2, tiled=True),
        lax.all_gather(w_up, "replica", axis=2, tiled=True),
        lax.all_gather(w_down, "replica", axis=1, tiled=True),
    )
    proj_local = proj_full[0]
    up_local = up_full[0]
    down_local = down_full[0]
    seed_full, loss_full = (
        lax.all_gather(incoming, "tensor", axis=2, tiled=True),
        lax.all_gather(loss_grads, "tensor", axis=2, tiled=True),
    )
    encoder = section_index < section_count // 2
    decoder_flag = jnp.where(encoder, 0.0, 1.0).astype(jnp.bfloat16)
    skip_mask = jnp.stack([jnp.ones((), jnp.bfloat16), decoder_flag])[None, :, None]
    encoder_weight = jnp.where(encoder, 1.0, 0.0).astype(jnp.float32)
    is_top = section_index == section_count - 1
    tick_count = crop_ids.shape[1]
    upstream = seed_full[0]
    kept_inputs, kept_mixed, kept_active, kept_hidden, kept_grads, kept_upstream = (
        [],
        [],
        [],
        [],
        [],
        [],
    )
    input_grad = None
    for tick_index in range(tick_count):
        picked_rows = crop_ids[0, tick_index]
        inputs = pool_inputs[0][picked_rows] * skip_mask
        mixed_rows = pool_mixed[0][picked_rows]
        pre_gelu = jnp.dot(mixed_rows, up_local, preferred_element_type=jnp.float32)
        gelu_value, gelu_slope = gelu_pair(pre_gelu)
        activated = gelu_value.astype(jnp.bfloat16)
        back_act = jnp.einsum("md,fd->mf", upstream, down_local, preferred_element_type=jnp.float32)
        back_hidden = (back_act * gelu_slope).astype(jnp.bfloat16)
        partial_back = jnp.einsum(
            "mf,df->md", back_hidden, up_local, preferred_element_type=jnp.float32
        )
        back_mixed = upstream.astype(jnp.float32) + lax.psum(partial_back, "tensor")
        mixed_grad = back_mixed.astype(jnp.bfloat16)
        input_grad = jnp.einsum(
            "mj,kij->mki", mixed_grad, proj_local, preferred_element_type=jnp.float32
        ).astype(jnp.bfloat16)
        kept_inputs.append(inputs)
        kept_mixed.append(mixed_rows)
        kept_active.append(activated)
        kept_hidden.append(back_hidden)
        kept_grads.append(mixed_grad)
        kept_upstream.append(upstream)
        if tick_index + 1 < tick_count:
            payload = lax.all_gather(input_grad, "tensor", axis=2, tiled=True)
            from_above = shifted(payload[:, 0], "section", -1)
            mirrored = reflect(payload[:, 1], section_count)
            summed = (
                from_above.astype(jnp.float32) + encoder_weight * mirrored.astype(jnp.float32)
            ).astype(jnp.bfloat16)
            upstream = jnp.where(is_top, loss_full[tick_index], summed)
    all_inputs = jnp.concatenate(kept_inputs, axis=0)
    all_mixed = jnp.concatenate(kept_mixed, axis=0)
    all_active = jnp.concatenate(kept_active, axis=0)
    all_hidden = jnp.concatenate(kept_hidden, axis=0)
    all_grads = jnp.concatenate(kept_grads, axis=0)
    all_upstream = jnp.concatenate(kept_upstream, axis=0)
    down_total = jnp.einsum(
        "mf,md->fd", all_active, all_upstream, preferred_element_type=jnp.float32
    )
    up_total = jnp.einsum("md,mf->df", all_mixed, all_hidden, preferred_element_type=jnp.float32)
    proj_total = jnp.einsum(
        "mki,mj->kij", all_inputs, all_grads, preferred_element_type=jnp.float32
    )
    reduced = (
        lax.psum_scatter(
            proj_total[None].astype(jnp.bfloat16), "replica", scatter_dimension=2, tiled=True
        ).astype(jnp.float32),
        lax.psum_scatter(
            up_total[None].astype(jnp.bfloat16), "replica", scatter_dimension=2, tiled=True
        ).astype(jnp.float32),
        lax.psum_scatter(
            down_total[None].astype(jnp.bfloat16), "replica", scatter_dimension=1, tiled=True
        ).astype(jnp.float32),
    )
    return (
        reduced[0].astype(jnp.bfloat16),
        reduced[1].astype(jnp.bfloat16),
        reduced[2].astype(jnp.bfloat16),
        input_grad[None],
    )


def solution(mesh):
    in_specs = (
        P("section", "replica", None, "tensor"),
        P("section", "replica", None),
        P("section", "replica", None),
        P("section", "replica", "tensor"),
        P(None, "replica", "tensor"),
        P("section", None, ("tensor", "replica"), None),
        P("section", None, ("tensor", "replica")),
        P("section", ("tensor", "replica"), None),
    )
    out_specs = (
        P("section", None, ("tensor", "replica"), None),
        P("section", None, ("tensor", "replica")),
        P("section", ("tensor", "replica"), None),
        P("section", "replica", None, "tensor"),
    )
    return jax.shard_map(body, mesh=mesh, in_specs=in_specs, out_specs=out_specs, check_vma=False)
```

profile of v0, /device:TPU:1, one launch (start us, length us, event | category | flops | bytes accessed | tf_op | source)
XLA Modules:
  0.0 1007.1 jit_solution(8471942278215179916)
XLA Ops:
  9.7 23.1 %all_gather.24 = bf16[1,128,1408]{1,2,0:T(8,128)(2,1)S(1)} all-gather(bf16[1,128,176]{1,2,0:T(8,128)(2,1)S(1)} %copy-done.36), channel_id=1, replica_groups=mesh['section'=32,'tensor'=8,'replica'=2] {'tensor'}, dimensions={2}, use_global_device_ids=true | all-gather | bytes 405504 | tf_op jit(solution)/shard_map/all_gather | solution.py:50
  32.8 16.5 %all-gather.6.cloned.1.call-done = bf16[1,1408,384]{1,2,0:T(8,128)(2,1)} async-done(((bf16[1,1408,192]{1,2,0:T(8,128)(2,1)}), bf16[1,1408,384]{1,2,0:T(8,128)(2,1)}) %all-gather.6.cloned.1.call-update) | async-done | bytes 1081360 | tf_op jit(solution)/shard_map/all_gather | solution.py:43
  51.7 33.1 %all-gather.4.cloned.1.call-done = bf16[1,384,1408]{2,1,0:T(8,128)(2,1)} async-done(((bf16[1,192,1408]{2,1,0:T(8,128)(2,1)}), bf16[1,384,1408]{2,1,0:T(8,128)(2,1)}) %all-gather.4.cloned.1.call-update) | async-done | bytes 1081360 | tf_op jit(solution)/shard_map/all_gather | solution.py:44
  89.5 14.4 %all_gather.28 = bf16[1,2,176,1408]{3,2,1,0:T(8,128)(2,1)S(1)} all-gather(bf16[1,2,88,1408]{3,2,1,0:T(8,128)(2,1)S(1)} %copy-done.23), channel_id=1, replica_groups=mesh['section'=32,'tensor'=8,'replica'=2] {'replica'}, dimensions={2}, use_global_device_ids=true | all-gather | bytes 1486848 | tf_op jit(solution)/shard_map/all_gather | solution.py:42
  103.8 70.2 %all-reduce.5.cloned.1.call-done = f32[128,1408]{1,0:T(8,128)} async-done(((f32[128,1408]{1,0:T(8,128)}), f32[128,1408]{1,0:T(8,128)}) %all-reduce.5.cloned.1.call-update) | async-done | bytes 720912 | tf_op jit(solution)/shard_map/psum | solution.py:81
  176.0 23.6 %all_gather.29 = bf16[128,2,1408]{0,1,2:T(2,128)(2,1)S(1)} all-gather(bf16[128,2,176]{0,1,2:T(2,128)(2,1)S(1)} %copy.36), channel_id=1, replica_groups=mesh['section'=32,'tensor'=8,'replica'=2] {'tensor'}, dimensions={2}, use_global_device_ids=true | all-gather | bytes 811008 | tf_op jit(solution)/shard_map/all_gather | solution.py:93
  204.3 14.3 %collective-permute-start.1 = (bf16[128,1408]{1,0:T(8,128)(2,1)}, bf16[128,1408]{1,0:T(8,128)(2,1)S(1)}, u32[]{:S(2)}, u32[]{:S(2)}) collective-permute-start(bf16[128,1408]{1,0:T(8,128)(2,1)} %bitcast.141), channel_id=1, source_target_pairs={{0,16},{16,0},{32,48},{48,32},{64,80},{80,64},{96,112},{112,96},{1... | collective-permute-start | bytes 1081352 | tf_op jit(solution)/shard_map/ppermute | solution.py:13
  223.2 8.4 collective-permute-done.2
  236.3 16.0 %collective-permute-done.3 = bf16[128,1408]{1,0:T(8,128)(2,1)} collective-permute-done((bf16[128,1408]{1,0:T(8,128)(2,1)}, bf16[128,1408]{1,0:T(8,128)(2,1)}, u32[]{:S(2)}, u32[]{:S(2)}) %collective-permute-start.3) | collective-permute-done | bytes 360480 | tf_op jit(solution)/shard_map/ppermute | solution.py:13
  268.7 22.2 %collective-permute-done.4 = bf16[128,1408]{1,0:T(8,128)(2,1)} collective-permute-done((bf16[128,1408]{1,0:T(8,128)(2,1)}, bf16[128,1408]{1,0:T(8,128)(2,1)}, u32[]{:S(2)}, u32[]{:S(2)}) %collective-permute-start.4) | collective-permute-done | bytes 360480 | tf_op jit(solution)/shard_map/ppermute | solution.py:13
  290.9 18.8 %collective-permute-start.5 = (bf16[128,1408]{1,0:T(8,128)(2,1)}, bf16[128,1408]{1,0:T(8,128)(2,1)}, u32[]{:S(2)}, u32[]{:S(2)}) collective-permute-start(bf16[128,1408]{1,0:T(8,128)(2,1)} %collective-permute-done.4), channel_id=1, source_target_pairs={{0,256},{16,272},{32,288},{48,304},{64,320},{80,336},{96,352},{112... | collective-permute-start | bytes 1081352 | tf_op jit(solution)/shard_map/ppermute | solution.py:13
  312.2 12.0 %collective-permute-done.5 = bf16[128,1408]{1,0:T(8,128)(2,1)} collective-permute-done((bf16[128,1408]{1,0:T(8,128)(2,1)}, bf16[128,1408]{1,0:T(8,128)(2,1)}, u32[]{:S(2)}, u32[]{:S(2)}) %collective-permute-start.5) | collective-permute-done | bytes 360480 | tf_op jit(solution)/shard_map/ppermute | solution.py:13
  327.9 87.2 %all-reduce.7.cloned.1.call-done = f32[128,1408]{1,0:T(8,128)} async-done(((f32[128,1408]{1,0:T(8,128)}), f32[128,1408]{1,0:T(8,128)}) %all-reduce.7.cloned.1.call-update) | async-done | bytes 720912 | tf_op jit(solution)/shard_map/psum | solution.py:81
  417.0 23.3 %all_gather.30 = bf16[128,2,1408]{0,1,2:T(2,128)(2,1)S(1)} all-gather(bf16[128,2,176]{0,1,2:T(2,128)(2,1)S(1)} %copy.40), channel_id=1, replica_groups=mesh['section'=32,'tensor'=8,'replica'=2] {'tensor'}, dimensions={2}, use_global_device_ids=true | all-gather | bytes 811008 | tf_op jit(solution)/shard_map/all_gather | solution.py:93
  444.9 13.9 %collective-permute-start.7 = (bf16[128,1408]{1,0:T(8,128)(2,1)}, bf16[128,1408]{1,0:T(8,128)(2,1)S(1)}, u32[]{:S(2)}, u32[]{:S(2)}) collective-permute-start(bf16[128,1408]{1,0:T(8,128)(2,1)} %bitcast.142), channel_id=1, source_target_pairs={{0,16},{16,0},{32,48},{48,32},{64,80},{80,64},{96,112},{112,96},{1... | collective-permute-start | bytes 1081352 | tf_op jit(solution)/shard_map/ppermute | solution.py:13
  463.3 8.5 collective-permute-done.8
  475.9 16.0 %collective-permute-done.9 = bf16[128,1408]{1,0:T(8,128)(2,1)} collective-permute-done((bf16[128,1408]{1,0:T(8,128)(2,1)S(1)}, bf16[128,1408]{1,0:T(8,128)(2,1)}, u32[]{:S(2)}, u32[]{:S(2)}) %collective-permute-start.9) | collective-permute-done | bytes 360480 | tf_op jit(solution)/shard_map/ppermute | solution.py:13
  504.4 26.1 %collective-permute-done.10 = bf16[128,1408]{1,0:T(8,128)(2,1)} collective-permute-done((bf16[128,1408]{1,0:T(8,128)(2,1)}, bf16[128,1408]{1,0:T(8,128)(2,1)}, u32[]{:S(2)}, u32[]{:S(2)}) %collective-permute-start.10) | collective-permute-done | bytes 360480 | tf_op jit(solution)/shard_map/ppermute | solution.py:13
  530.4 18.7 %collective-permute-start.11 = (bf16[128,1408]{1,0:T(8,128)(2,1)}, bf16[128,1408]{1,0:T(8,128)(2,1)}, u32[]{:S(2)}, u32[]{:S(2)}) collective-permute-start(bf16[128,1408]{1,0:T(8,128)(2,1)} %collective-permute-done.10), channel_id=1, source_target_pairs={{0,256},{16,272},{32,288},{48,304},{64,320},{80,336},{96,352},{112... | collective-permute-start | bytes 1081352 | tf_op jit(solution)/shard_map/ppermute | solution.py:13
  551.5 12.0 %collective-permute-done.11 = bf16[128,1408]{1,0:T(8,128)(2,1)} collective-permute-done((bf16[128,1408]{1,0:T(8,128)(2,1)}, bf16[128,1408]{1,0:T(8,128)(2,1)}, u32[]{:S(2)}, u32[]{:S(2)}) %collective-permute-start.11) | collective-permute-done | bytes 360480 | tf_op jit(solution)/shard_map/ppermute | solution.py:13
  566.6 86.3 %all-reduce.9.cloned.1.call-done = f32[128,1408]{1,0:T(8,128)} async-done(((f32[128,1408]{1,0:T(8,128)}), f32[128,1408]{1,0:T(8,128)}) %all-reduce.9.cloned.1.call-update) | async-done | bytes 720912 | tf_op jit(solution)/shard_map/psum | solution.py:81
  654.8 23.3 %all_gather.31 = bf16[128,2,1408]{0,1,2:T(2,128)(2,1)S(1)} all-gather(bf16[128,2,176]{0,1,2:T(2,128)(2,1)S(1)} %copy.44), channel_id=1, replica_groups=mesh['section'=32,'tensor'=8,'replica'=2] {'tensor'}, dimensions={2}, use_global_device_ids=true | all-gather | bytes 811008 | tf_op jit(solution)/shard_map/all_gather | solution.py:93
  682.7 13.9 %collective-permute-start.13 = (bf16[128,1408]{1,0:T(8,128)(2,1)}, bf16[128,1408]{1,0:T(8,128)(2,1)S(1)}, u32[]{:S(2)}, u32[]{:S(2)}) collective-permute-start(bf16[128,1408]{1,0:T(8,128)(2,1)} %bitcast.143), channel_id=1, source_target_pairs={{0,16},{16,0},{32,48},{48,32},{64,80},{80,64},{96,112},{112,96},{1... | collective-permute-start | bytes 1081352 | tf_op jit(solution)/shard_map/ppermute | solution.py:13
  701.1 8.5 collective-permute-done.14
  713.6 16.0 %collective-permute-done.15 = bf16[128,1408]{1,0:T(8,128)(2,1)} collective-permute-done((bf16[128,1408]{1,0:T(8,128)(2,1)S(1)}, bf16[128,1408]{1,0:T(8,128)(2,1)}, u32[]{:S(2)}, u32[]{:S(2)}) %collective-permute-start.15) | collective-permute-done | bytes 360480 | tf_op jit(solution)/shard_map/ppermute | solution.py:13
  742.3 25.9 %collective-permute-done.16 = bf16[128,1408]{1,0:T(8,128)(2,1)} collective-permute-done((bf16[128,1408]{1,0:T(8,128)(2,1)}, bf16[128,1408]{1,0:T(8,128)(2,1)}, u32[]{:S(2)}, u32[]{:S(2)}) %collective-permute-start.16) | collective-permute-done | bytes 360480 | tf_op jit(solution)/shard_map/ppermute | solution.py:13
  768.2 18.7 %collective-permute-start.17 = (bf16[128,1408]{1,0:T(8,128)(2,1)}, bf16[128,1408]{1,0:T(8,128)(2,1)}, u32[]{:S(2)}, u32[]{:S(2)}) collective-permute-start(bf16[128,1408]{1,0:T(8,128)(2,1)} %collective-permute-done.16), channel_id=1, source_target_pairs={{0,256},{16,272},{32,288},{48,304},{64,320},{80,336},{96,352},{112... | collective-permute-start | bytes 1081352 | tf_op jit(solution)/shard_map/ppermute | solution.py:13
  789.3 12.0 %collective-permute-done.17 = bf16[128,1408]{1,0:T(8,128)(2,1)} collective-permute-done((bf16[128,1408]{1,0:T(8,128)(2,1)}, bf16[128,1408]{1,0:T(8,128)(2,1)}, u32[]{:S(2)}, u32[]{:S(2)}) %collective-permute-start.17) | collective-permute-done | bytes 360480 | tf_op jit(solution)/shard_map/ppermute | solution.py:13
  823.1 68.8 %all-reduce.11.cloned.1.call-done = f32[128,1408]{1,0:T(8,128)} async-done(((f32[128,1408]{1,0:T(8,128)}), f32[128,1408]{1,0:T(8,128)}) %all-reduce.11.cloned.1.call-update) | async-done | bytes 720912 | tf_op jit(solution)/shard_map/psum | solution.py:81
  901.8 29.7 %reduce-scatter.12.cloned.1.call-done = bf16[192,1408]{1,0:T(8,128)(2,1)} async-done(((bf16[384,1408]{1,0:T(8,128)(2,1)}), bf16[192,1408]{1,0:T(8,128)(2,1)}) %reduce-scatter.12.cloned.1.call-update) | async-done | bytes 540688
  933.9 31.3 %reduce-scatter.10.cloned.1.call-done = bf16[88,2816]{1,0:T(8,128)(2,1)} async-done(((bf16[176,2816]{1,0:T(8,128)(2,1)}), bf16[88,2816]{1,0:T(8,128)(2,1)}) %reduce-scatter.10.cloned.1.call-update) | async-done | bytes 495632
  967.2 33.1 %reduce-scatter.8.cloned.1.call-done = bf16[1,192,1408]{2,1,0:T(8,128)(2,1)} async-done(((bf16[1,384,1408]{2,1,0:T(8,128)(2,1)}), bf16[1,192,1408]{2,1,0:T(8,128)(2,1)}) %reduce-scatter.8.cloned.1.call-update) | async-done | bytes 540688 | tf_op jit(solution)/shard_map/reduce_scatter | solution.py:120
  (192 shorter events, 146.5 us)
Async XLA Ops:
  7.2 42.2 %all-gather.6.cloned.1.call-start = ((), (), s32[]{:S(2)}) async-start(), calls=%async_computation.4 | async-start | bytes 1622016 | tf_op jit(solution)/shard_map/all_gather | solution.py:43
  7.9 76.9 %all-gather.4.cloned.1.call-start = ((), (), s32[]{:S(2)}) async-start(), calls=%async_computation.3 | async-start | bytes 1622016 | tf_op jit(solution)/shard_map/all_gather | solution.py:44
  8.7 165.4 %all-reduce.5.cloned.1.call-start = ((), (), s32[]{:S(2)}) async-start(), calls=%async_computation.5 | async-start | bytes 1441792 | tf_op jit(solution)/shard_map/psum | solution.py:81
  9.7 76.9 %copy-start.6 = (bf16[128,1408]{1,0:T(8,128)(2,1)}, bf16[128,1408]{1,0:T(8,128)(2,1)S(1)}, u32[]{:S(2)}) copy-start(bf16[128,1408]{1,0:T(8,128)(2,1)S(1)} %gather_fusion.4) | copy-start | bytes 1081348
  88.5 221.3 %all-gather.8.cloned.1.call-start = ((), (), s32[]{:S(2)}) async-start(), calls=%async_computation.6 | async-start | bytes 1216512 | tf_op jit(solution)/shard_map/all_gather | solution.py:51
  89.1 326.0 %all-reduce.7.cloned.1.call-start = ((), (), s32[]{:S(2)}) async-start(), calls=%async_computation.7 | async-start | bytes 1441792 | tf_op jit(solution)/shard_map/psum | solution.py:81
  204.3 15.8 %collective-permute-start.1 = (bf16[128,1408]{1,0:T(8,128)(2,1)}, bf16[128,1408]{1,0:T(8,128)(2,1)S(1)}, u32[]{:S(2)}, u32[]{:S(2)}) collective-permute-start(bf16[128,1408]{1,0:T(8,128)(2,1)} %bitcast.141), channel_id=1, source_target_pairs={{0,16},{16,0},{32,48},{48,32},{64,80},{80,64},{96,112},{112,96},{1... | collective-permute-start | bytes 1081352 | tf_op jit(solution)/shard_map/ppermute | solution.py:13
  220.1 11.6 %collective-permute-start.2 = (bf16[128,1408]{1,0:T(8,128)(2,1)S(1)}, bf16[128,1408]{1,0:T(8,128)(2,1)}, u32[]{:S(2)}, u32[]{:S(2)}) collective-permute-start(bf16[128,1408]{1,0:T(8,128)(2,1)S(1)} %collective-permute-done.1), channel_id=1, source_target_pairs={{0,32},{16,48},{32,0},{48,16},{64,96},{80,112},{96,64},{112,80},{1... | collective-permute-start | bytes 1081352 | tf_op jit(solution)/shard_map/ppermute | solution.py:13
  231.7 20.6 %collective-permute-start.3 = (bf16[128,1408]{1,0:T(8,128)(2,1)}, bf16[128,1408]{1,0:T(8,128)(2,1)}, u32[]{:S(2)}, u32[]{:S(2)}) collective-permute-start(bf16[128,1408]{1,0:T(8,128)(2,1)} %collective-permute-done.2), channel_id=1, source_target_pairs={{0,64},{16,80},{32,96},{48,112},{64,0},{80,16},{96,32},{112,48},{1... | collective-permute-start | bytes 1081352 | tf_op jit(solution)/shard_map/ppermute | solution.py:13
  252.3 38.6 %collective-permute-start.4 = (bf16[128,1408]{1,0:T(8,128)(2,1)}, bf16[128,1408]{1,0:T(8,128)(2,1)}, u32[]{:S(2)}, u32[]{:S(2)}) collective-permute-start(bf16[128,1408]{1,0:T(8,128)(2,1)} %collective-permute-done.3), channel_id=1, source_target_pairs={{0,128},{16,144},{32,160},{48,176},{64,192},{80,208},{96,224},{112... | collective-permute-start | bytes 1081352 | tf_op jit(solution)/shard_map/ppermute | solution.py:13
  265.0 47.2 %collective-permute-start = (bf16[128,1408]{1,0:T(8,128)(2,1)}, bf16[128,1408]{1,0:T(8,128)(2,1)}, u32[]{:S(2)}, u32[]{:S(2)}) collective-permute-start(bf16[128,1408]{1,0:T(8,128)(2,1)} %bitcast.138), channel_id=1, source_target_pairs={{16,0},{32,16},{48,32},{64,48},{80,64},{96,80},{112,96},{128,112},... | collective-permute-start | bytes 1081352 | tf_op jit(solution)/shard_map/ppermute | solution.py:19
  290.9 33.2 %collective-permute-start.5 = (bf16[128,1408]{1,0:T(8,128)(2,1)}, bf16[128,1408]{1,0:T(8,128)(2,1)}, u32[]{:S(2)}, u32[]{:S(2)}) collective-permute-start(bf16[128,1408]{1,0:T(8,128)(2,1)} %collective-permute-done.4), channel_id=1, source_target_pairs={{0,256},{16,272},{32,288},{48,304},{64,320},{80,336},{96,352},{112... | collective-permute-start | bytes 1081352 | tf_op jit(solution)/shard_map/ppermute | solution.py:13
  325.4 89.7 %copy-start.8 = (bf16[128,1408]{1,0:T(8,128)(2,1)}, bf16[128,1408]{1,0:T(8,128)(2,1)S(1)}, u32[]{:S(2)}) copy-start(bf16[128,1408]{1,0:T(8,128)(2,1)S(1)} %fusion.66) | copy-start | bytes 1081348
  327.9 325.0 %all-reduce.9.cloned.1.call-start = ((), (), s32[]{:S(2)}) async-start(), calls=%async_computation.8 | async-start | bytes 1441792 | tf_op jit(solution)/shard_map/psum | solution.py:81
  444.9 15.4 %collective-permute-start.7 = (bf16[128,1408]{1,0:T(8,128)(2,1)}, bf16[128,1408]{1,0:T(8,128)(2,1)S(1)}, u32[]{:S(2)}, u32[]{:S(2)}) collective-permute-start(bf16[128,1408]{1,0:T(8,128)(2,1)} %bitcast.142), channel_id=1, source_target_pairs={{0,16},{16,0},{32,48},{48,32},{64,80},{80,64},{96,112},{112,96},{1... | collective-permute-start | bytes 1081352 | tf_op jit(solution)/shard_map/ppermute | solution.py:13
  460.3 11.5 %collective-permute-start.8 = (bf16[128,1408]{1,0:T(8,128)(2,1)S(1)}, bf16[128,1408]{1,0:T(8,128)(2,1)S(1)}, u32[]{:S(2)}, u32[]{:S(2)}) collective-permute-start(bf16[128,1408]{1,0:T(8,128)(2,1)S(1)} %collective-permute-done.7), channel_id=1, source_target_pairs={{0,32},{16,48},{32,0},{48,16},{64,96},{80,112},{96,64},{112,80},{1... | collective-permute-start | bytes 1081352 | tf_op jit(solution)/shard_map/ppermute | solution.py:13
  471.8 20.1 %collective-permute-start.9 = (bf16[128,1408]{1,0:T(8,128)(2,1)S(1)}, bf16[128,1408]{1,0:T(8,128)(2,1)}, u32[]{:S(2)}, u32[]{:S(2)}) collective-permute-start(bf16[128,1408]{1,0:T(8,128)(2,1)S(1)} %collective-permute-done.8), channel_id=1, source_target_pairs={{0,64},{16,80},{32,96},{48,112},{64,0},{80,16},{96,32},{112,48},{1... | collective-permute-start | bytes 1081352 | tf_op jit(solution)/shard_map/ppermute | solution.py:13
  491.9 38.5 %collective-permute-start.10 = (bf16[128,1408]{1,0:T(8,128)(2,1)}, bf16[128,1408]{1,0:T(8,128)(2,1)}, u32[]{:S(2)}, u32[]{:S(2)}) collective-permute-start(bf16[128,1408]{1,0:T(8,128)(2,1)} %collective-permute-done.9), channel_id=1, source_target_pairs={{0,128},{16,144},{32,160},{48,176},{64,192},{80,208},{96,224},{112... | collective-permute-start | bytes 1081352 | tf_op jit(solution)/shard_map/ppermute | solution.py:13
  500.6 50.9 %collective-permute-start.6 = (bf16[128,1408]{1,0:T(8,128)(2,1)}, bf16[128,1408]{1,0:T(8,128)(2,1)}, u32[]{:S(2)}, u32[]{:S(2)}) collective-permute-start(bf16[128,1408]{1,0:T(8,128)(2,1)} %bitcast.140), channel_id=1, source_target_pairs={{16,0},{32,16},{48,32},{64,48},{80,64},{96,80},{112,96},{128,112},... | collective-permute-start | bytes 1081352 | tf_op jit(solution)/shard_map/ppermute | solution.py:19
  530.4 33.0 %collective-permute-start.11 = (bf16[128,1408]{1,0:T(8,128)(2,1)}, bf16[128,1408]{1,0:T(8,128)(2,1)}, u32[]{:S(2)}, u32[]{:S(2)}) collective-permute-start(bf16[128,1408]{1,0:T(8,128)(2,1)} %collective-permute-done.10), channel_id=1, source_target_pairs={{0,256},{16,272},{32,288},{48,304},{64,320},{80,336},{96,352},{112... | collective-permute-start | bytes 1081352 | tf_op jit(solution)/shard_map/ppermute | solution.py:13
  564.8 88.1 %copy-start.13 = (bf16[128,1408]{1,0:T(8,128)(2,1)}, bf16[128,1408]{1,0:T(8,128)(2,1)S(1)}, u32[]{:S(2)}) copy-start(bf16[128,1408]{1,0:T(8,128)(2,1)S(1)} %fusion.67) | copy-start | bytes 1081348
  566.6 325.3 %all-reduce.11.cloned.1.call-start = ((), (), s32[]{:S(2)}) async-start(), calls=%async_computation.9 | async-start | bytes 1441792 | tf_op jit(solution)/shard_map/psum | solution.py:81
  682.7 15.4 %collective-permute-start.13 = (bf16[128,1408]{1,0:T(8,128)(2,1)}, bf16[128,1408]{1,0:T(8,128)(2,1)S(1)}, u32[]{:S(2)}, u32[]{:S(2)}) collective-permute-start(bf16[128,1408]{1,0:T(8,128)(2,1)} %bitcast.143), channel_id=1, source_target_pairs={{0,16},{16,0},{32,48},{48,32},{64,80},{80,64},{96,112},{112,96},{1... | collective-permute-start | bytes 1081352 | tf_op jit(solution)/shard_map/ppermute | solution.py:13
  698.1 11.5 %collective-permute-start.14 = (bf16[128,1408]{1,0:T(8,128)(2,1)S(1)}, bf16[128,1408]{1,0:T(8,128)(2,1)S(1)}, u32[]{:S(2)}, u32[]{:S(2)}) collective-permute-start(bf16[128,1408]{1,0:T(8,128)(2,1)S(1)} %collective-permute-done.13), channel_id=1, source_target_pairs={{0,32},{16,48},{32,0},{48,16},{64,96},{80,112},{96,64},{112,80},{1... | collective-permute-start | bytes 1081352 | tf_op jit(solution)/shard_map/ppermute | solution.py:13
  709.6 20.1 %collective-permute-start.15 = (bf16[128,1408]{1,0:T(8,128)(2,1)S(1)}, bf16[128,1408]{1,0:T(8,128)(2,1)}, u32[]{:S(2)}, u32[]{:S(2)}) collective-permute-start(bf16[128,1408]{1,0:T(8,128)(2,1)S(1)} %collective-permute-done.14), channel_id=1, source_target_pairs={{0,64},{16,80},{32,96},{48,112},{64,0},{80,16},{96,32},{112,48},{1... | collective-permute-start | bytes 1081352 | tf_op jit(solution)/shard_map/ppermute | solution.py:13
  729.7 38.5 %collective-permute-start.16 = (bf16[128,1408]{1,0:T(8,128)(2,1)}, bf16[128,1408]{1,0:T(8,128)(2,1)}, u32[]{:S(2)}, u32[]{:S(2)}) collective-permute-start(bf16[128,1408]{1,0:T(8,128)(2,1)} %collective-permute-done.15), channel_id=1, source_target_pairs={{0,128},{16,144},{32,160},{48,176},{64,192},{80,208},{96,224},{112... | collective-permute-start | bytes 1081352 | tf_op jit(solution)/shard_map/ppermute | solution.py:13
  738.6 50.7 %collective-permute-start.12 = (bf16[128,1408]{1,0:T(8,128)(2,1)}, bf16[128,1408]{1,0:T(8,128)(2,1)}, u32[]{:S(2)}, u32[]{:S(2)}) collective-permute-start(bf16[128,1408]{1,0:T(8,128)(2,1)} %bitcast.139), channel_id=1, source_target_pairs={{16,0},{32,16},{48,32},{64,48},{80,64},{96,80},{112,96},{128,112},... | collective-permute-start | bytes 1081352 | tf_op jit(solution)/shard_map/ppermute | solution.py:19
  768.2 33.0 %collective-permute-start.17 = (bf16[128,1408]{1,0:T(8,128)(2,1)}, bf16[128,1408]{1,0:T(8,128)(2,1)}, u32[]{:S(2)}, u32[]{:S(2)}) collective-permute-start(bf16[128,1408]{1,0:T(8,128)(2,1)} %collective-permute-done.16), channel_id=1, source_target_pairs={{0,256},{16,272},{32,288},{48,304},{64,320},{80,336},{96,352},{112... | collective-permute-start | bytes 1081352 | tf_op jit(solution)/shard_map/ppermute | solution.py:13
  805.7 125.8 %reduce-scatter.12.cloned.1.call-start = ((), (), s32[]{:S(2)}) async-start(), calls=%async_computation.12 | async-start | bytes 1622016
  815.5 149.6 %reduce-scatter.10.cloned.1.call-start = ((), (), s32[]{:S(2)}) async-start(), calls=%async_computation.11 | async-start | bytes 1486848
  818.3 73.6 %copy-start.19 = (bf16[128,1408]{1,0:T(8,128)(2,1)S(1)}, bf16[128,1408]{1,0:T(8,128)(2,1)}, u32[]{:S(2)}) copy-start(bf16[128,1408]{1,0:T(8,128)(2,1)} %copy-done.18) | copy-start | bytes 1081348
  896.5 103.8 %reduce-scatter.8.cloned.1.call-start = ((), (), s32[]{:S(2)}) async-start(), calls=%async_computation.10 | async-start | bytes 1622016 | tf_op jit(solution)/shard_map/reduce_scatter | solution.py:120
  (37 other events, 366.3 us)
Sparse Core Ops, SparseCore 0:
  10.1 39.1 all-gather.5
  51.4 33.3 all-gather.3
  88.6 85.4 all-reduce.4
  176.0 49.4 all-gather.7
  328.0 87.0 all-reduce.6
  566.7 86.1 all-reduce.8
  805.8 86.0 all-reduce.10
  894.7 36.7 reduce-scatter.11
  934.2 30.8 reduce-scatter.9
  968.4 31.8 reduce-scatter.7
where the time goes:
time: 1010 us
  waiting for transfers between devices  646 us (64%)
  starting transfers between devices  153 us (15%)
  blocking collectives  108 us (11%)
  local copies, waits for them, and re-layouts  51.2 us (5%)
  matrix products  23.4 us (2%)
  between operations  14.9 us (1%)
  other arithmetic  10.5 us (1%)
    psum x4, waiting for transfers between devices, body(): back_mixed = upstream.astype(jnp.float32) + lax.psum(partial_back, 'tensor')  312 us
    ppermute x15, waiting for transfers between devices, from_partner(): return lax.ppermute(value, axis, pairs)  188 us
    ppermute x15, starting transfers between devices, from_partner(): return lax.ppermute(value, axis, pairs)  141 us
    all_gather x3, blocking collectives, body(): payload = lax.all_gather(input_grad, 'tensor', axis=2, tiled=True)  70.2 us
    unnamed x12, waiting for transfers between devices  63 us
    unnamed x100, local copies, waits for them, and re-layouts  34.3 us
    reduce_scatter x1, waiting for transfers between devices, body(): lax.psum_scatter(down_total[None].astype(jnp.bfloat16), 'replica', scatte...  33.1 us
    all_gather x1, waiting for transfers between devices, body(): lax.all_gather(w_down, 'replica', axis=1, tiled=True)  33.1 us
  transfers between devices with their start and end apart: 28, of which 24 were waited for; matrix products, arithmetic and copies ran while one was open for 5% of the time, Pallas kernels for 0%

commit v1 on v0

--- a/solution.py
+++ b/solution.py
@@ -90,7 +90,10 @@
         kept_grads.append(mixed_grad)
         kept_upstream.append(upstream)
         if tick_index + 1 < tick_count:
-            payload = lax.all_gather(input_grad, "tensor", axis=2, tiled=True)
+            payload = jnp.concatenate(
+                lax.all_to_all(jnp.stack([input_grad] * lax.axis_size("tensor")), "tensor", 0, 0),
+                axis=2,
+            )
             from_above = shifted(payload[:, 0], "section", -1)
             mirrored = reflect(payload[:, 1], section_count)
             summed = (

time: 1010 us -> 953 us (0.944)
  blocking collectives: 108 us -> 59 us
  starting transfers between devices: 153 us -> 141 us
    all_gather x3 -> x0, blocking collectives: 70.2 us -> none  [body(): payload = lax.all_gather(input_grad, 'tensor', axis=2, tiled=True)]
    all_to_all x0 -> x2, blocking collectives: none -> 21.5 us  [body(): lax.all_to_all(jnp.stack([input_grad] * lax.axis_size('tensor')), 'tensor...]
    ppermute x15, starting transfers between devices: 141 us -> 126 us  [from_partner(): return lax.ppermute(value, axis, pairs)]
    unnamed x100 -> x96, local copies, waits for them, and re-layouts: 34.3 us -> 34.5 us
  transfers between devices with their start and end apart: 28 -> 29, of which waited for: 24 -> 25; matrix products, arithmetic and copies ran while one was open for 5% -> 5% of each run, Pallas kernels for 0% -> 0%
where the time goes in v1:
time: 953 us; the launch traced here: 951 us
  waiting for transfers between devices  655 us (69%)
  starting transfers between devices  141 us (15%)
  blocking collectives  59 us (6%)
  local copies, waits for them, and re-layouts  48.2 us (5%)
  matrix products  23.4 us (2%)
  between operations  14.9 us (2%)
  other arithmetic  9.75 us (1%)
    psum x4, waiting for transfers between devices, body(): back_mixed = upstream.astype(jnp.float32) + lax.psum(partial_back, 'tensor')  315 us
    ppermute x15, waiting for transfers between devices, from_partner(): return lax.ppermute(value, axis, pairs)  187 us
    ppermute x15, starting transfers between devices, from_partner(): return lax.ppermute(value, axis, pairs)  126 us
    unnamed x12, waiting for transfers between devices  63 us
    unnamed x96, local copies, waits for them, and re-layouts  34.5 us
    reduce_scatter x1, waiting for transfers between devices, body(): lax.psum_scatter(down_total[None].astype(jnp.bfloat16), 'replica', scatte...  33.1 us
    all_gather x1, waiting for transfers between devices, body(): lax.all_gather(w_down, 'replica', axis=1, tiled=True)  33.1 us
    all_gather x1, blocking collectives, body(): lax.all_gather(incoming, 'tensor', axis=2, tiled=True)  23.1 us
  transfers between devices with their start and end apart: 29, of which 25 were waited for; matrix products, arithmetic and copies ran while one was open for 5% of the time, Pallas kernels for 0%

profile of v1, /device:TPU:1, one launch (start us, length us, event | category | flops | bytes accessed | tf_op | source)
XLA Modules:
  0.0 951.2 jit_solution(9283304016955087848)
XLA Ops:
  9.7 23.1 %all_gather.15 = bf16[1,128,1408]{1,2,0:T(8,128)(2,1)S(1)} all-gather(bf16[1,128,176]{1,2,0:T(8,128)(2,1)S(1)} %copy-done.34), channel_id=1, replica_groups=mesh['section'=32,'tensor'=8,'replica'=2] {'tensor'}, dimensions={2}, use_global_device_ids=true | all-gather | bytes 405504 | tf_op jit(solution)/shard_map/all_gather | solution.py:50
  32.8 16.5 %all-gather.6.cloned.1.call-done = bf16[1,1408,384]{1,2,0:T(8,128)(2,1)} async-done(((bf16[1,1408,192]{1,2,0:T(8,128)(2,1)}), bf16[1,1408,384]{1,2,0:T(8,128)(2,1)}) %all-gather.6.cloned.1.call-update) | async-done | bytes 1081360 | tf_op jit(solution)/shard_map/all_gather | solution.py:43
  51.7 33.1 %all-gather.4.cloned.1.call-done = bf16[1,384,1408]{2,1,0:T(8,128)(2,1)} async-done(((bf16[1,192,1408]{2,1,0:T(8,128)(2,1)}), bf16[1,384,1408]{2,1,0:T(8,128)(2,1)}) %all-gather.4.cloned.1.call-update) | async-done | bytes 1081360 | tf_op jit(solution)/shard_map/all_gather | solution.py:44
  88.9 14.3 %all_gather.19 = bf16[1,2,176,1408]{3,2,1,0:T(8,128)(2,1)S(1)} all-gather(bf16[1,2,88,1408]{3,2,1,0:T(8,128)(2,1)S(1)} %copy-done.21), channel_id=1, replica_groups=mesh['section'=32,'tensor'=8,'replica'=2] {'replica'}, dimensions={2}, use_global_device_ids=true | all-gather | bytes 1486848 | tf_op jit(solution)/shard_map/all_gather | solution.py:42
  103.2 70.2 %all-reduce.5.cloned.1.call-done = f32[128,1408]{1,0:T(8,128)} async-done(((f32[128,1408]{1,0:T(8,128)}), f32[128,1408]{1,0:T(8,128)}) %all-reduce.5.cloned.1.call-update) | async-done | bytes 720912 | tf_op jit(solution)/shard_map/psum | solution.py:81
  181.0 7.3 all-to-all-done
  189.3 8.7 collective-permute-start.1
  202.7 8.5 collective-permute-done.2
  215.3 15.8 %collective-permute-done.3 = bf16[128,1408]{1,0:T(8,128)(2,1)} collective-permute-done((bf16[128,1408]{1,0:T(8,128)(2,1)S(1)}, bf16[128,1408]{1,0:T(8,128)(2,1)}, u32[]{:S(2)}, u32[]{:S(2)}) %collective-permute-start.3) | collective-permute-done | bytes 360480 | tf_op jit(solution)/shard_map/ppermute | solution.py:13
  245.1 24.5 %collective-permute-done.4 = bf16[128,1408]{1,0:T(8,128)(2,1)} collective-permute-done((bf16[128,1408]{1,0:T(8,128)(2,1)}, bf16[128,1408]{1,0:T(8,128)(2,1)}, u32[]{:S(2)}, u32[]{:S(2)}) %collective-permute-start.4) | collective-permute-done | bytes 360480 | tf_op jit(solution)/shard_map/ppermute | solution.py:13
  269.6 18.9 %collective-permute-start.5 = (bf16[128,1408]{1,0:T(8,128)(2,1)}, bf16[128,1408]{1,0:T(8,128)(2,1)}, u32[]{:S(2)}, u32[]{:S(2)}) collective-permute-start(bf16[128,1408]{1,0:T(8,128)(2,1)} %collective-permute-done.4), channel_id=1, source_target_pairs={{0,256},{16,272},{32,288},{48,304},{64,320},{80,336},{96,352},{112... | collective-permute-start | bytes 1081352 | tf_op jit(solution)/shard_map/ppermute | solution.py:13
  292.5 10.6 %collective-permute-done.5 = bf16[128,1408]{1,0:T(8,128)(2,1)} collective-permute-done((bf16[128,1408]{1,0:T(8,128)(2,1)}, bf16[128,1408]{1,0:T(8,128)(2,1)}, u32[]{:S(2)}, u32[]{:S(2)}) %collective-permute-start.5) | collective-permute-done | bytes 360480 | tf_op jit(solution)/shard_map/ppermute | solution.py:13
  307.6 86.6 %all-reduce.7.cloned.1.call-done = f32[128,1408]{1,0:T(8,128)} async-done(((f32[128,1408]{1,0:T(8,128)}), f32[128,1408]{1,0:T(8,128)}) %all-reduce.7.cloned.1.call-update) | async-done | bytes 720912 | tf_op jit(solution)/shard_map/psum | solution.py:81
  396.8 10.8 %all_to_all.15 = bf16[8,128,2,176]{1,3,2,0:T(8,128)(2,1)S(1)} all-to-all(bf16[8,128,2,176]{1,3,2,0:T(8,128)(2,1)S(1)} %stack.13), channel_id=1, replica_groups=mesh['section'=32,'tensor'=8,'replica'=2] {'tensor'}, dimensions={0} | all-to-all | bytes 1441792 | tf_op jit(solution)/shard_map/all_to_all | solution.py:94
  410.4 8.9 collective-permute-start.7
  423.9 8.5 collective-permute-done.8
  436.4 16.0 %collective-permute-done.9 = bf16[128,1408]{1,0:T(8,128)(2,1)} collective-permute-done((bf16[128,1408]{1,0:T(8,128)(2,1)S(1)}, bf16[128,1408]{1,0:T(8,128)(2,1)}, u32[]{:S(2)}, u32[]{:S(2)}) %collective-permute-start.9) | collective-permute-done | bytes 360480 | tf_op jit(solution)/shard_map/ppermute | solution.py:13
  465.1 25.8 %collective-permute-done.10 = bf16[128,1408]{1,0:T(8,128)(2,1)} collective-permute-done((bf16[128,1408]{1,0:T(8,128)(2,1)}, bf16[128,1408]{1,0:T(8,128)(2,1)}, u32[]{:S(2)}, u32[]{:S(2)}) %collective-permute-start.10) | collective-permute-done | bytes 360480 | tf_op jit(solution)/shard_map/ppermute | solution.py:13
  490.9 18.7 %collective-permute-start.11 = (bf16[128,1408]{1,0:T(8,128)(2,1)}, bf16[128,1408]{1,0:T(8,128)(2,1)}, u32[]{:S(2)}, u32[]{:S(2)}) collective-permute-start(bf16[128,1408]{1,0:T(8,128)(2,1)} %collective-permute-done.10), channel_id=1, source_target_pairs={{0,256},{16,272},{32,288},{48,304},{64,320},{80,336},{96,352},{112... | collective-permute-start | bytes 1081352 | tf_op jit(solution)/shard_map/ppermute | solution.py:13
  514.4 9.6 %collective-permute-done.11 = bf16[128,1408]{1,0:T(8,128)(2,1)} collective-permute-done((bf16[128,1408]{1,0:T(8,128)(2,1)}, bf16[128,1408]{1,0:T(8,128)(2,1)}, u32[]{:S(2)}, u32[]{:S(2)}) %collective-permute-start.11) | collective-permute-done | bytes 360480 | tf_op jit(solution)/shard_map/ppermute | solution.py:13
  527.8 87.0 %all-reduce.9.cloned.1.call-done = f32[128,1408]{1,0:T(8,128)} async-done(((f32[128,1408]{1,0:T(8,128)}), f32[128,1408]{1,0:T(8,128)}) %all-reduce.9.cloned.1.call-update) | async-done | bytes 720912 | tf_op jit(solution)/shard_map/psum | solution.py:81
  617.3 10.8 %all_to_all.16 = bf16[8,128,2,176]{1,3,2,0:T(8,128)(2,1)S(1)} all-to-all(bf16[8,128,2,176]{1,3,2,0:T(8,128)(2,1)S(1)} %stack.14), channel_id=1, replica_groups=mesh['section'=32,'tensor'=8,'replica'=2] {'tensor'}, dimensions={0} | all-to-all | bytes 1441792 | tf_op jit(solution)/shard_map/all_to_all | solution.py:94
  630.8 8.9 collective-permute-start.13
  644.3 8.5 collective-permute-done.14
  656.8 16.0 %collective-permute-done.15 = bf16[128,1408]{1,0:T(8,128)(2,1)} collective-permute-done((bf16[128,1408]{1,0:T(8,128)(2,1)S(1)}, bf16[128,1408]{1,0:T(8,128)(2,1)}, u32[]{:S(2)}, u32[]{:S(2)}) %collective-permute-start.15) | collective-permute-done | bytes 360480 | tf_op jit(solution)/shard_map/ppermute | solution.py:13
  684.5 26.8 %collective-permute-done.16 = bf16[128,1408]{1,0:T(8,128)(2,1)} collective-permute-done((bf16[128,1408]{1,0:T(8,128)(2,1)}, bf16[128,1408]{1,0:T(8,128)(2,1)}, u32[]{:S(2)}, u32[]{:S(2)}) %collective-permute-start.16) | collective-permute-done | bytes 360480 | tf_op jit(solution)/shard_map/ppermute | solution.py:13
  711.3 18.9 %collective-permute-start.17 = (bf16[128,1408]{1,0:T(8,128)(2,1)}, bf16[128,1408]{1,0:T(8,128)(2,1)}, u32[]{:S(2)}, u32[]{:S(2)}) collective-permute-start(bf16[128,1408]{1,0:T(8,128)(2,1)} %collective-permute-done.16), channel_id=1, source_target_pairs={{0,256},{16,272},{32,288},{48,304},{64,320},{80,336},{96,352},{112... | collective-permute-start | bytes 1081352 | tf_op jit(solution)/shard_map/ppermute | solution.py:13
  732.6 11.8 %collective-permute-done.17 = bf16[128,1408]{1,0:T(8,128)(2,1)} collective-permute-done((bf16[128,1408]{1,0:T(8,128)(2,1)}, bf16[128,1408]{1,0:T(8,128)(2,1)}, u32[]{:S(2)}, u32[]{:S(2)}) %collective-permute-start.17) | collective-permute-done | bytes 360480 | tf_op jit(solution)/shard_map/ppermute | solution.py:13
  764.7 71.2 %all-reduce.11.cloned.1.call-done = f32[128,1408]{1,0:T(8,128)} async-done(((f32[128,1408]{1,0:T(8,128)}), f32[128,1408]{1,0:T(8,128)}) %all-reduce.11.cloned.1.call-update) | async-done | bytes 720912 | tf_op jit(solution)/shard_map/psum | solution.py:81
  845.8 29.7 %reduce-scatter.12.cloned.1.call-done = bf16[192,1408]{1,0:T(8,128)(2,1)} async-done(((bf16[384,1408]{1,0:T(8,128)(2,1)}), bf16[192,1408]{1,0:T(8,128)(2,1)}) %reduce-scatter.12.cloned.1.call-update) | async-done | bytes 540688
  878.0 31.3 %reduce-scatter.10.cloned.1.call-done = bf16[88,2816]{1,0:T(8,128)(2,1)} async-done(((bf16[176,2816]{1,0:T(8,128)(2,1)}), bf16[88,2816]{1,0:T(8,128)(2,1)}) %reduce-scatter.10.cloned.1.call-update) | async-done | bytes 495632
  911.2 33.1 %reduce-scatter.8.cloned.1.call-done = bf16[1,192,1408]{2,1,0:T(8,128)(2,1)} async-done(((bf16[1,384,1408]{2,1,0:T(8,128)(2,1)}), bf16[1,192,1408]{2,1,0:T(8,128)(2,1)}) %reduce-scatter.8.cloned.1.call-update) | async-done | bytes 540688 | tf_op jit(solution)/shard_map/reduce_scatter | solution.py:123
  (192 shorter events, 145.8 us)
Async XLA Ops:
  7.2 42.2 %all-gather.6.cloned.1.call-start = ((), (), s32[]{:S(2)}) async-start(), calls=%async_computation.7 | async-start | bytes 1622016 | tf_op jit(solution)/shard_map/all_gather | solution.py:43
  7.9 76.9 %all-gather.4.cloned.1.call-start = ((), (), s32[]{:S(2)}) async-start(), calls=%async_computation.6 | async-start | bytes 1622016 | tf_op jit(solution)/shard_map/all_gather | solution.py:44
  8.7 164.8 %all-reduce.5.cloned.1.call-start = ((), (), s32[]{:S(2)}) async-start(), calls=%async_computation.8 | async-start | bytes 1441792 | tf_op jit(solution)/shard_map/psum | solution.py:81
  9.7 76.9 %copy-start.4 = (bf16[128,1408]{1,0:T(8,128)(2,1)}, bf16[128,1408]{1,0:T(8,128)(2,1)S(1)}, u32[]{:S(2)}) copy-start(bf16[128,1408]{1,0:T(8,128)(2,1)S(1)} %gather_fusion.4) | copy-start | bytes 1081348
  176.8 11.5 %all-to-all-start = ((bf16[8,128,2,176]{1,3,2,0:T(8,128)(2,1)}), bf16[8,128,2,176]{1,3,2,0:T(8,128)(2,1)S(1)}, u32[]{:S(2)}, u32[]{:S(2)}) async-start(bf16[8,128,2,176]{1,3,2,0:T(8,128)(2,1)} %stack.12), calls=%async_computation | async-start | bytes 1441792 | tf_op jit(solution)/shard_map/all_to_all | solution.py:94
  180.4 108.2 %all-gather.8.cloned.1.call-start = ((), (), s32[]{:S(2)}) async-start(), calls=%async_computation.9 | async-start | bytes 1216512 | tf_op jit(solution)/shard_map/all_gather | solution.py:51
  180.9 213.3 %all-reduce.7.cloned.1.call-start = ((), (), s32[]{:S(2)}) async-start(), calls=%async_computation.10 | async-start | bytes 1441792 | tf_op jit(solution)/shard_map/psum | solution.py:81
  189.3 10.2 %collective-permute-start.1 = (bf16[128,1408]{1,0:T(8,128)(2,1)}, bf16[128,1408]{1,0:T(8,128)(2,1)S(1)}, u32[]{:S(2)}, u32[]{:S(2)}) collective-permute-start(bf16[128,1408]{1,0:T(8,128)(2,1)} %bitcast.153), channel_id=1, source_target_pairs={{0,16},{16,0},{32,48},{48,32},{64,80},{80,64},{96,112},{112,96},{1... | collective-permute-start | bytes 1081352 | tf_op jit(solution)/shard_map/ppermute | solution.py:13
  199.5 11.6 %collective-permute-start.2 = (bf16[128,1408]{1,0:T(8,128)(2,1)S(1)}, bf16[128,1408]{1,0:T(8,128)(2,1)S(1)}, u32[]{:S(2)}, u32[]{:S(2)}) collective-permute-start(bf16[128,1408]{1,0:T(8,128)(2,1)S(1)} %collective-permute-done.1), channel_id=1, source_target_pairs={{0,32},{16,48},{32,0},{48,16},{64,96},{80,112},{96,64},{112,80},{1... | collective-permute-start | bytes 1081352 | tf_op jit(solution)/shard_map/ppermute | solution.py:13
  211.1 19.9 %collective-permute-start.3 = (bf16[128,1408]{1,0:T(8,128)(2,1)S(1)}, bf16[128,1408]{1,0:T(8,128)(2,1)}, u32[]{:S(2)}, u32[]{:S(2)}) collective-permute-start(bf16[128,1408]{1,0:T(8,128)(2,1)S(1)} %collective-permute-done.2), channel_id=1, source_target_pairs={{0,64},{16,80},{32,96},{48,112},{64,0},{80,16},{96,32},{112,48},{1... | collective-permute-start | bytes 1081352 | tf_op jit(solution)/shard_map/ppermute | solution.py:13
  231.0 38.6 %collective-permute-start.4 = (bf16[128,1408]{1,0:T(8,128)(2,1)}, bf16[128,1408]{1,0:T(8,128)(2,1)}, u32[]{:S(2)}, u32[]{:S(2)}) collective-permute-start(bf16[128,1408]{1,0:T(8,128)(2,1)} %collective-permute-done.3), channel_id=1, source_target_pairs={{0,128},{16,144},{32,160},{48,176},{64,192},{80,208},{96,224},{112... | collective-permute-start | bytes 1081352 | tf_op jit(solution)/shard_map/ppermute | solution.py:13
  241.4 51.1 %collective-permute-start = (bf16[128,1408]{1,0:T(8,128)(2,1)}, bf16[128,1408]{1,0:T(8,128)(2,1)}, u32[]{:S(2)}, u32[]{:S(2)}) collective-permute-start(bf16[128,1408]{1,0:T(8,128)(2,1)} %bitcast.150), channel_id=1, source_target_pairs={{16,0},{32,16},{48,32},{64,48},{80,64},{96,80},{112,96},{128,112},... | collective-permute-start | bytes 1081352 | tf_op jit(solution)/shard_map/ppermute | solution.py:19
  269.6 33.4 %collective-permute-start.5 = (bf16[128,1408]{1,0:T(8,128)(2,1)}, bf16[128,1408]{1,0:T(8,128)(2,1)}, u32[]{:S(2)}, u32[]{:S(2)}) collective-permute-start(bf16[128,1408]{1,0:T(8,128)(2,1)} %collective-permute-done.4), channel_id=1, source_target_pairs={{0,256},{16,272},{32,288},{48,304},{64,320},{80,336},{96,352},{112... | collective-permute-start | bytes 1081352 | tf_op jit(solution)/shard_map/ppermute | solution.py:13
  307.6 307.3 %all-reduce.9.cloned.1.call-start = ((), (), s32[]{:S(2)}) async-start(), calls=%async_computation.11 | async-start | bytes 1441792 | tf_op jit(solution)/shard_map/psum | solution.py:81
  410.4 10.4 %collective-permute-start.7 = (bf16[128,1408]{1,0:T(8,128)(2,1)}, bf16[128,1408]{1,0:T(8,128)(2,1)S(1)}, u32[]{:S(2)}, u32[]{:S(2)}) collective-permute-start(bf16[128,1408]{1,0:T(8,128)(2,1)} %bitcast.154), channel_id=1, source_target_pairs={{0,16},{16,0},{32,48},{48,32},{64,80},{80,64},{96,112},{112,96},{1... | collective-permute-start | bytes 1081352 | tf_op jit(solution)/shard_map/ppermute | solution.py:13
  420.8 11.5 %collective-permute-start.8 = (bf16[128,1408]{1,0:T(8,128)(2,1)S(1)}, bf16[128,1408]{1,0:T(8,128)(2,1)S(1)}, u32[]{:S(2)}, u32[]{:S(2)}) collective-permute-start(bf16[128,1408]{1,0:T(8,128)(2,1)S(1)} %collective-permute-done.7), channel_id=1, source_target_pairs={{0,32},{16,48},{32,0},{48,16},{64,96},{80,112},{96,64},{112,80},{1... | collective-permute-start | bytes 1081352 | tf_op jit(solution)/shard_map/ppermute | solution.py:13
  432.3 20.0 %collective-permute-start.9 = (bf16[128,1408]{1,0:T(8,128)(2,1)S(1)}, bf16[128,1408]{1,0:T(8,128)(2,1)}, u32[]{:S(2)}, u32[]{:S(2)}) collective-permute-start(bf16[128,1408]{1,0:T(8,128)(2,1)S(1)} %collective-permute-done.8), channel_id=1, source_target_pairs={{0,64},{16,80},{32,96},{48,112},{64,0},{80,16},{96,32},{112,48},{1... | collective-permute-start | bytes 1081352 | tf_op jit(solution)/shard_map/ppermute | solution.py:13
  452.4 38.5 %collective-permute-start.10 = (bf16[128,1408]{1,0:T(8,128)(2,1)}, bf16[128,1408]{1,0:T(8,128)(2,1)}, u32[]{:S(2)}, u32[]{:S(2)}) collective-permute-start(bf16[128,1408]{1,0:T(8,128)(2,1)} %collective-permute-done.9), channel_id=1, source_target_pairs={{0,128},{16,144},{32,160},{48,176},{64,192},{80,208},{96,224},{112... | collective-permute-start | bytes 1081352 | tf_op jit(solution)/shard_map/ppermute | solution.py:13
  461.3 53.0 %collective-permute-start.6 = (bf16[128,1408]{1,0:T(8,128)(2,1)}, bf16[128,1408]{1,0:T(8,128)(2,1)}, u32[]{:S(2)}, u32[]{:S(2)}) collective-permute-start(bf16[128,1408]{1,0:T(8,128)(2,1)} %bitcast.152), channel_id=1, source_target_pairs={{16,0},{32,16},{48,32},{64,48},{80,64},{96,80},{112,96},{128,112},... | collective-permute-start | bytes 1081352 | tf_op jit(solution)/shard_map/ppermute | solution.py:19
  490.9 33.1 %collective-permute-start.11 = (bf16[128,1408]{1,0:T(8,128)(2,1)}, bf16[128,1408]{1,0:T(8,128)(2,1)}, u32[]{:S(2)}, u32[]{:S(2)}) collective-permute-start(bf16[128,1408]{1,0:T(8,128)(2,1)} %collective-permute-done.10), channel_id=1, source_target_pairs={{0,256},{16,272},{32,288},{48,304},{64,320},{80,336},{96,352},{112... | collective-permute-start | bytes 1081352 | tf_op jit(solution)/shard_map/ppermute | solution.py:13
  525.4 89.5 %copy-start.12 = (bf16[128,1408]{1,0:T(8,128)(2,1)}, bf16[128,1408]{1,0:T(8,128)(2,1)S(1)}, u32[]{:S(2)}) copy-start(bf16[128,1408]{1,0:T(8,128)(2,1)S(1)} %fusion.67) | copy-start | bytes 1081348
  527.8 308.1 %all-reduce.11.cloned.1.call-start = ((), (), s32[]{:S(2)}) async-start(), calls=%async_computation.12 | async-start | bytes 1441792 | tf_op jit(solution)/shard_map/psum | solution.py:81
  630.8 10.4 %collective-permute-start.13 = (bf16[128,1408]{1,0:T(8,128)(2,1)}, bf16[128,1408]{1,0:T(8,128)(2,1)S(1)}, u32[]{:S(2)}, u32[]{:S(2)}) collective-permute-start(bf16[128,1408]{1,0:T(8,128)(2,1)} %bitcast.155), channel_id=1, source_target_pairs={{0,16},{16,0},{32,48},{48,32},{64,80},{80,64},{96,112},{112,96},{1... | collective-permute-start | bytes 1081352 | tf_op jit(solution)/shard_map/ppermute | solution.py:13
  641.3 11.5 %collective-permute-start.14 = (bf16[128,1408]{1,0:T(8,128)(2,1)S(1)}, bf16[128,1408]{1,0:T(8,128)(2,1)S(1)}, u32[]{:S(2)}, u32[]{:S(2)}) collective-permute-start(bf16[128,1408]{1,0:T(8,128)(2,1)S(1)} %collective-permute-done.13), channel_id=1, source_target_pairs={{0,32},{16,48},{32,0},{48,16},{64,96},{80,112},{96,64},{112,80},{1... | collective-permute-start | bytes 1081352 | tf_op jit(solution)/shard_map/ppermute | solution.py:13
  652.8 20.0 %collective-permute-start.15 = (bf16[128,1408]{1,0:T(8,128)(2,1)S(1)}, bf16[128,1408]{1,0:T(8,128)(2,1)}, u32[]{:S(2)}, u32[]{:S(2)}) collective-permute-start(bf16[128,1408]{1,0:T(8,128)(2,1)S(1)} %collective-permute-done.14), channel_id=1, source_target_pairs={{0,64},{16,80},{32,96},{48,112},{64,0},{80,16},{96,32},{112,48},{1... | collective-permute-start | bytes 1081352 | tf_op jit(solution)/shard_map/ppermute | solution.py:13
  672.8 38.5 %collective-permute-start.16 = (bf16[128,1408]{1,0:T(8,128)(2,1)}, bf16[128,1408]{1,0:T(8,128)(2,1)}, u32[]{:S(2)}, u32[]{:S(2)}) collective-permute-start(bf16[128,1408]{1,0:T(8,128)(2,1)} %collective-permute-done.15), channel_id=1, source_target_pairs={{0,128},{16,144},{32,160},{48,176},{64,192},{80,208},{96,224},{112... | collective-permute-start | bytes 1081352 | tf_op jit(solution)/shard_map/ppermute | solution.py:13
  680.8 51.8 %collective-permute-start.12 = (bf16[128,1408]{1,0:T(8,128)(2,1)}, bf16[128,1408]{1,0:T(8,128)(2,1)}, u32[]{:S(2)}, u32[]{:S(2)}) collective-permute-start(bf16[128,1408]{1,0:T(8,128)(2,1)} %bitcast.151), channel_id=1, source_target_pairs={{16,0},{32,16},{48,32},{64,48},{80,64},{96,80},{112,96},{128,112},... | collective-permute-start | bytes 1081352 | tf_op jit(solution)/shard_map/ppermute | solution.py:19
  711.3 33.2 %collective-permute-start.17 = (bf16[128,1408]{1,0:T(8,128)(2,1)}, bf16[128,1408]{1,0:T(8,128)(2,1)}, u32[]{:S(2)}, u32[]{:S(2)}) collective-permute-start(bf16[128,1408]{1,0:T(8,128)(2,1)} %collective-permute-done.16), channel_id=1, source_target_pairs={{0,256},{16,272},{32,288},{48,304},{64,320},{80,336},{96,352},{112... | collective-permute-start | bytes 1081352 | tf_op jit(solution)/shard_map/ppermute | solution.py:13
  748.9 126.6 %reduce-scatter.12.cloned.1.call-start = ((), (), s32[]{:S(2)}) async-start(), calls=%async_computation.15 | async-start | bytes 1622016
  758.8 150.5 %reduce-scatter.10.cloned.1.call-start = ((), (), s32[]{:S(2)}) async-start(), calls=%async_computation.14 | async-start | bytes 1486848
  761.5 74.4 %copy-start.17 = (bf16[128,1408]{1,0:T(8,128)(2,1)S(1)}, bf16[128,1408]{1,0:T(8,128)(2,1)}, u32[]{:S(2)}) copy-start(bf16[128,1408]{1,0:T(8,128)(2,1)} %copy-done.16) | copy-start | bytes 1081348
  840.5 103.9 %reduce-scatter.8.cloned.1.call-start = ((), (), s32[]{:S(2)}) async-start(), calls=%async_computation.13 | async-start | bytes 1622016 | tf_op jit(solution)/shard_map/reduce_scatter | solution.py:123
  (36 other events, 647.8 us)
Sparse Core Ops, SparseCore 0:
  10.1 39.1 all-gather.5
  51.4 33.3 all-gather.3
  88.0 85.4 all-reduce.4
  183.0 48.8 all-gather.7
  307.7 86.5 all-reduce.6
  527.9 86.9 all-reduce.8
  749.0 86.8 all-reduce.10
  838.7 36.7 reduce-scatter.11
  878.3 30.8 reduce-scatter.9
  912.5 31.8 reduce-scatter.7
